TPU v7x, 32 devices: a whole 2x2x4 slice. The times are simulated.
32 devices in a mesh: dp: 4 (over y, core), fsdp: 8 (over z, x).
Axes of the slice: x: 2, y: 2, z: 4, core: 2. Of those that a mesh axis runs over, the one named last changes fastest.
Arguments:
- dec_in: bfloat16 [2, 32, 128, 768], P(None, ('dp', 'fsdp')), may hold values from -6 to 6
- enc_out: bfloat16 [2, 32, 512, 768], P(None, ('dp', 'fsdp')), may hold values from -6 to 6
- dec_len: int32 [2, 32], P(None, ('dp', 'fsdp')), may hold values from 1 to 114, as said below
- enc_len: int32 [2, 32], P(None, ('dp', 'fsdp')), may hold values from 32 to 512, as said below
- cotangent: bfloat16 [2, 32, 128, 768], P(None, ('dp', 'fsdp')), may hold values from -6 to 6
- norm_self: bfloat16 [768], P(('dp', 'fsdp')), may hold values from 0.5 to 1.5
- self_q: bfloat16 [768, 768], P(('dp', 'fsdp')), may hold values from -0.109375 to 0.109375
- self_k: bfloat16 [768, 768], P(('dp', 'fsdp')), may hold values from -0.109375 to 0.109375
- self_v: bfloat16 [768, 768], P(('dp', 'fsdp')), may hold values from -0.21875 to 0.21875
- self_o: bfloat16 [768, 768], P(('dp', 'fsdp')), may hold values from -0.625 to 0.625
- rel_bias: bfloat16 [32, 12], P('fsdp'), may hold values from -4 to 4
- norm_cross: bfloat16 [768], P(('dp', 'fsdp')), may hold values from 0.5 to 1.5
- cross_q: bfloat16 [768, 768], P(('dp', 'fsdp')), may hold values from -0.109375 to 0.109375
- cross_k: bfloat16 [768, 768], P(('dp', 'fsdp')), may hold values from -0.109375 to 0.109375
- cross_v: bfloat16 [768, 768], P(('dp', 'fsdp')), may hold values from -0.21875 to 0.21875
- cross_o: bfloat16 [768, 768], P(('dp', 'fsdp')), may hold values from -1.25 to 1.25
- norm_ffn: bfloat16 [768], P(('dp', 'fsdp')), may hold values from 0.5 to 1.5
- ffn_in: bfloat16 [768, 3072], P(('dp', 'fsdp')), may hold values from -0.21875 to 0.21875
- ffn_out: bfloat16 [3072, 768], P(('dp', 'fsdp')), may hold values from -0.15625 to 0.15625
Outputs:
- output: bfloat16 [2, 32, 128, 768], P(None, ('dp', 'fsdp'))
- grad_dec: bfloat16 [2, 32, 128, 768], P(None, ('dp', 'fsdp'))
- grad_enc: bfloat16 [2, 32, 512, 768], P(None, ('dp', 'fsdp'))
- grad_norm_self: float32 [768], P(('dp', 'fsdp'))
- grad_self_q: float32 [768, 768], P(('dp', 'fsdp'))
- grad_self_k: float32 [768, 768], P(('dp', 'fsdp'))
- grad_self_v: float32 [768, 768], P(('dp', 'fsdp'))
- grad_self_o: float32 [768, 768], P(('dp', 'fsdp'))
- grad_rel_bias: float32 [32, 12], P('fsdp')
- grad_norm_cross: float32 [768], P(('dp', 'fsdp'))
- grad_cross_q: float32 [768, 768], P(('dp', 'fsdp'))
- grad_cross_k: float32 [768, 768], P(('dp', 'fsdp'))
- grad_cross_v: float32 [768, 768], P(('dp', 'fsdp'))
- grad_cross_o: float32 [768, 768], P(('dp', 'fsdp'))
- grad_norm_ffn: float32 [768], P(('dp', 'fsdp'))
- grad_ffn_in: float32 [768, 3072], P(('dp', 'fsdp'))
- grad_ffn_out: float32 [3072, 768], P(('dp', 'fsdp'))
Inputs may be any that keep to these rules, and one draw needn't show every extreme that they name: `dec_len`: every micro-batch has some target of exactly 114. `enc_len`: every micro-batch has some encoder input of exactly 512.
All inputs are finite; a program needn't handle non-finite values.
Results may differ from a plain program's by a relative error of at most 0.024.
The roundings to bfloat16 on the way count: a program that leaves them out, or rounds other values in their place, can miss the bound.
Values may be sent and summed in bfloat16 or wider, within the bound.
A program may use at most 256 MiB of HBM per device.

v0:
```python
import functools
import math

import jax
import jax.numpy as jnp
import numpy as np
from jax import lax
from jax.experimental import pallas as pl
from jax.experimental.pallas import tpu as pltpu
from jax.sharding import PartitionSpec as P

MESH = pl.DeviceIdType.MESH
NP = 8
ROWS = 48
COLS = 768
ALL = slice(None)


class Place:
    def __init__(s):
        dp, f = lax.axis_index("dp"), lax.axis_index("fsdp")
        s.c, s.y, s.x, s.z = dp % 2, dp // 2, f % 2, f // 2
        s.pos = {"x": s.x, "y": s.y, "z": s.z}

    def dev(s, c=None, y=None, z=None, x=None):
        c = s.c if c is None else c
        y = s.y if y is None else y
        z = s.z if z is None else z
        x = s.x if x is None else x
        return (y * 2 + c, z * 2 + x)

    def core(s):
        return s.dev(c=1 - s.c)

    def over(s, axis, j=1):
        if axis == "x":
            return s.dev(x=1 - s.x)
        if axis == "y":
            return s.dev(y=1 - s.y)
        return s.dev(z=(s.z + j) % 4)

    def others(s):
        return [s.over("x"), s.over("y")] + [s.over("z", j) for j in (1, 2, 3)]


def signal(sem, dev):
    pl.semaphore_signal(sem, inc=1, device_id=dev, device_id_type=MESH)


def greet(me):
    for d in me.others() + [me.core()]:
        signal(pltpu.get_barrier_semaphore(), d)


def all_here():
    pl.semaphore_wait(pltpu.get_barrier_semaphore(), 6)


class Mover:
    def __init__(s, me, ss, rs, rows):
        s.me, s.ss, s.rs, s.rows, s.sent = me, ss, rs, rows, []

    def copy(s, u, slot, src, dst, dev):
        return pltpu.make_async_remote_copy(
            src_ref=src, dst_ref=dst, send_sem=s.ss.at[s.rows[u], slot], recv_sem=s.rs.at[s.rows[u], slot],
            device_id=dev, device_id_type=MESH,
        )

    def send(s, *what):
        cp = s.copy(*what)
        cp.start()
        s.sent.append((what[0], cp))

    def arrived(s, u, slot, dst):
        s.copy(u, slot, dst, dst, s.me.core()).wait_recv()

    def drain(s, us=None):
        for u, cp in s.sent:
            if us is None or u in us:
                cp.wait_send()
        s.sent = [] if us is None else [e for e in s.sent if e[0] not in us]


class Gather(Mover):
    def __init__(s, me, A, ss, rs, rows):
        super().__init__(me, ss, rs, rows)
        s.A = A

    def steps(s, u, b, c0, nc, order):
        me = s.me

        def region(done, c=me.c, **at):
            ix = {a: (at[a] if a in at else ALL if a in done else me.pos[a]) for a in "yzx"}
            return s.A.at[b, ix["y"], c, ix["z"], ix["x"], :, pl.ds(c0, nc)]

        def hop(a, done):
            if a == "z":
                for j in (3, 2, 1):
                    s.send(u, 2 + j, region(done), region(done), me.over(a, j))
            else:
                s.send(u, 1 if a == "x" else 2, region(done), region(done), me.over(a))

        def land(a, done):
            if a == "z":
                for j in (1, 2, 3):
                    s.arrived(u, 2 + j, region(done, z=(me.z + 4 - j) % 4))
            else:
                s.arrived(u, 1 if a == "x" else 2, region(done, **{a: 1 - me.pos[a]}))

        def step(k):
            if 0 < k < 4:
                land(order[k - 1], order[: k - 1])
            if k < 3:
                hop(order[k], order[:k])
            elif k == 3:
                s.send(u, 0, region(order), region(order), me.core())
            else:
                s.arrived(u, 0, region(order, c=1 - me.c))

        return [functools.partial(step, k) for k in range(5)]


class Reduce(Mover):
    def __init__(s, me, G, RC, out, ss, rs, rows, ready, free, slots, count):
        super().__init__(me, ss, rs, rows)
        s.G, s.RC, s.out, s.ready, s.free, s.slots, s.count = G, RC, out, ready, free, slots, count
        s.todo = {}

    def steps(s, u, p, g, c0, nc, order, units):
        me, G, oc = s.me, s.G, 1 - s.me.c
        cols = pl.ds(c0, nc)
        opened, added = s.todo.setdefault(p, ([], []))

        def region(done, **at):
            ix = {a: (at[a] if a in at else me.pos[a] if a in done else ALL) for a in "yzx"}
            return G.at[g, ix["y"], me.c, ix["z"], ix["x"], :, cols]

        def slot(k, z=None):
            i = {
                "xyz": ((ALL, ALL, 0), (0, ALL, 1), (1, z, 1)),
                "yxz": ((0, ALL, ALL), (1, ALL, 0), (1, z, 1)),
                "zyx": ((ALL, z, ALL), (0, me.z, ALL), (1, me.z, 0)),
                "zxy": ((ALL, z, ALL), (ALL, me.z, 0), (0, me.z, 1)),
            }[order][k]
            return G.at[g, i[0], oc, i[1], i[2], :, cols]

        def hop(k):
            a = order[k]
            if a == "z":
                for j in (3, 2, 1):
                    s.send(u, 2 + j, region(order[:k], z=(me.z + j) % 4), slot(k, me.z), me.over(a, j))
            else:
                s.send(u, 1 if a == "x" else 2, region(order[:k], **{a: 1 - me.pos[a]}), slot(k), me.over(a))

        def land(k):
            a = order[k]
            own = region(order[:k], **{a: me.pos[a]})
            if a == "z":
                got = [(2 + j, slot(k, (me.z + 4 - j) % 4)) for j in (1, 2, 3)]
            else:
                got = [(1 if a == "x" else 2, slot(k))]
            total = own[...].astype(jnp.float32)
            for n, ref in got:
                s.arrived(u, n, ref)
                total = total + ref[...].astype(jnp.float32)
            if k == 2:
                s.out[p, :, cols] = total
            else:
                own[...] = total.astype(jnp.bfloat16)

        def core():
            return s.copy(
                u, 0, G.at[g, :, oc, :, :, :, cols], s.RC.at[p % s.slots, :, :, :, :, cols], me.core()
            )

        def first():
            if p >= s.slots and p not in s.todo[-1]:
                pl.semaphore_wait(s.free.at[p], 1)
                s.todo[-1].add(p)
            core().start()

        def open_up():
            core().wait_send()
            opened.append(u)
            if len(opened) == units:
                for i, d in enumerate(me.others()):
                    signal(s.ready.at[p, i], d)

        def second():
            s.arrived(u, 0, s.RC.at[p % s.slots, :, :, :, :, cols])

            def add(i, carry):
                own = G.at[g, i // 4, me.c, i % 4, :, :, cols]
                got = s.RC.at[p % s.slots, i // 4, i % 4, :, :, cols]
                own[...] = (own[...].astype(jnp.float32) + got[...].astype(jnp.float32)).astype(jnp.bfloat16)
                return carry

            lax.fori_loop(0, 8, add, 0)
            if not added:
                for i in range(5):
                    pl.semaphore_wait(s.ready.at[p, i], 1)
            added.append(u)
            hop(0)
            if len(added) == units and p + s.slots < s.count:
                signal(s.free.at[p + s.slots], me.core())

        def later(k):
            land(k)
            if k < 2:
                hop(k + 1)

        s.todo.setdefault(-1, set())
        return [first, open_up, second] + [functools.partial(later, k) for k in range(3)]

WIDTH = 768
DEC = 128
ENC = 512
SEQS = 2
HERE = (4, 8, SEQS, DEC, ENC, WIDTH)
CHUNKS = (2, 2, 4, 2)
TROWS = 16
SLOTS = 4
OWN = WIDTH // 32
PAIRS = WIDTH // 128
HALF = WIDTH // 2
BLK = 256
RD = SEQS * DEC
RE = SEQS * ENC
GELU = math.sqrt(2.0 / math.pi)
PLACE = (9, 8, 10, 11, 4, 7, 5, 6)
GATHERED = (
    (1, 0, 128, "zyx"),
    (1, 128, 512, "zyx"),
    (1, 640, 128, "zyx"),
    (2, 0, 384, "zxy"),
    (2, 384, 256, "yzx"),
    (2, 640, 128, "zyx"),
    (3, 0, 256, "zxy"),
    (3, 256, 384, "zxy"),
    (3, 640, 128, "zyx"),
    (4, 0, 512, "xzy"),
    (4, 512, 128, "zyx"),
    (4, 640, 128, "zxy"),
    (5, 0, 384, "zyx"),
    (5, 384, 256, "xzy"),
    (5, 640, 128, "yxz"),
    (6, 0, 384, "yzx"),
    (6, 384, 256, "zyx"),
    (6, 640, 128, "xzy"),
    (7, 0, 512, "zxy"),
    (7, 512, 128, "xyz"),
    (7, 640, 128, "zyx"),
    (8, 0, 256, "zxy"),
    (8, 256, 256, "xyz"),
    (8, 512, 256, "zyx"),
)
REDUCED = (
    (0, 0, 384, "xyz"),
    (0, 384, 256, "yxz"),
    (0, 640, 128, "zxy"),
    (1, 0, 256, "xyz"),
    (1, 256, 384, "yxz"),
    (1, 640, 128, "zxy"),
    (2, 0, 640, "xyz"),
    (2, 640, 128, "zxy"),
    (3, 0, 640, "yxz"),
    (3, 640, 128, "zyx"),
    (4, 0, 384, "xyz"),
    (4, 384, 256, "yxz"),
    (4, 640, 128, "zyx"),
    (5, 0, 384, "xyz"),
    (5, 384, 256, "yxz"),
    (5, 640, 128, "zyx"),
    (6, 0, 256, "xyz"),
    (6, 256, 384, "yxz"),
    (6, 640, 128, "zyx"),
    (7, 0, 384, "xyz"),
    (7, 384, 384, "yxz"),
)
PLAN = (
    240, 2000, 90, 100, 110, 0, 10, 20, 60, 241, 70, 80, 91, 101, 242, 111,
    1, 102, 243, 112, 244, 2001, 11, 21, 2, 103, 2002, 61, 113, 104, 30, 40,
    50, 114, 71, 3, 81, 4, 12, 62, 22, 41, 82, 72, 150, 160, 170, 63,
    92, 64, 120, 130, 140, 31, 51, 13, 73, 180, 190, 200, 23, 14, 151, 74,
    24, 2003, 42, 83, 171, 131, 161, 2004, 84, 210, 220, 230, 32, 191, 121, 93,
    141, 52, 43, 94, 221, 181, 142, 162, 201, 44, 53, 54, 33, 182, 192, 152,
    34, 2005, 172, 2006, 122, 2007, 222, 163, 2008, 202, 2009, 132, 164, 2010, 2011, 2012,
    211, 2013, 2014, 2015, 231, 2016, 153, 2017, 2018, 2019, 154, 2020, 183, 2021, 143, 2022,
    173, 2023, 123, 144, 184, 2024, 174, 2025, 193, 124, 203, 133, 194, 212, 204, 134,
    2026, 232, 2027, 2028, 2029, 1000, 1010, 1020, 1001, 213, 1011, 1021, 223, 233, 1002, 214,
    1012, 1022, 224, 234, 2030, 2031, 2032, 2033, 1030, 1040, 1050, 2034, 1031, 2035, 2036, 1013,
    1041, 1051, 2037, 1060, 1070, 1080, 1090, 1003, 1032, 2038, 2039, 1061, 1023, 1071, 1042, 1052,
    1014, 1081, 1091, 2040, 1062, 1072, 1004, 1082, 1092, 1033, 1024, 2041, 2042, 2043, 2044, 2045,
    2046, 1043, 1053, 2047, 2048, 1015, 2049, 2050, 1100, 1110, 1120, 2051, 1101, 2052, 1063, 1073,
    1111, 1121, 2053, 1130, 1140, 1150, 1102, 1044, 1005, 1083, 1074, 1131, 1141, 1151, 1054, 1112,
    1122, 1034, 1025, 2054, 1132, 1142, 1152, 1093, 2055, 2056, 1075, 1064, 1045, 1055, 1103, 2057,
    2058, 2059, 2060, 2061, 1113, 1123, 1084, 1035, 1160, 1170, 1180, 2062, 1190, 1200, 1161, 2063,
    1171, 1181, 1143, 2064, 1094, 1191, 1162, 1153, 1201, 1172, 1182, 1133, 1192, 1104, 1202, 1154,
    1114, 1124, 2065, 2066, 1065, 1144, 1095, 2067, 2068, 2069, 1085, 1163, 1173, 1210, 1211, 1134,
    1183, 1212, 1193, 1155, 1125, 1105, 1115, 1203, 1174, 1213, 1145, 1164, 1184, 1135, 1194, 1204,
    1185, 1214, 1175, 1165, 1195, 1205, 1215,
)


def bucket_rows():
    table = bucket_table(DEC, NB)[:, 0]
    far = table[(-np.arange(DEC)) % DEC]
    rows = np.full((8, TROWS), -1)
    rows[:, 4:8] = np.arange(NB).reshape(8, 4)
    return jnp.asarray((rows.reshape(-1, 1) == far[None, :]).astype(np.float32), jnp.bfloat16)


def sem_rows(gathered, reduced):
    deep = [max(gathered.count(p), reduced.count(p)) for p in range(NP)]

    def rows(pieces):
        return [sum(deep[:p]) + pieces[:i].count(p) for i, p in enumerate(pieces)] + [sum(deep)]

    return rows(gathered), rows(reduced), sum(deep)


def loop(n, body):
    def step(i, carry):
        body(i)
        return carry

    lax.fori_loop(0, n, step, 0)


def tile(i, n):
    return pl.ds(pl.multiple_of(i * n, n), n)


def f32(v):
    return v.astype(jnp.float32)


def layer_kernel(
    dlen, elen, dec_hbm, enc_hbm, cot_hbm, small, bmap,
    sq, sk, sv, so, cq, ck, cv, co, fi, fo,
    out_hbm, gdec_hbm, genc_hbm, gw, gt,
    BUF, T, GT, RCT, RC,
    X, C, E, K, V, A1, Q1, K1, V1, O1, A2, Q2, O2, A3, GO, HID, GP,
    Y1, Y2, F2, GY, PS, PC, BIAS, NRM, DM,
    ss, rs, ready, free, tready, tfree, lsem,
):
    me = Place()
    greet(me)
    loads = [
        pltpu.make_async_copy(a, b, lsem.at[i])
        for i, (a, b) in enumerate(((dec_hbm, X), (cot_hbm, C), (enc_hbm, E)))
    ]
    for cp in loads:
        cp.start()

    def pack(p, top, bottom):
        both = jnp.concatenate([f32(top), f32(bottom)], axis=0)
        BUF[p + 1, me.y, me.c, me.z, me.x] = low(both)

    pack(0, sq[...], sk[...])
    pack(1, sv[...], so[...])
    pack(2, ck[...], cv[...])
    pack(3, cq[...], co[...])
    BUF[5, me.y, me.c, me.z, me.x] = fo[0:48]
    BUF[6, me.y, me.c, me.z, me.x] = fo[48:96]
    for h in range(2):
        pack(6 + h, fi[:, 1536 * h : 1536 * h + 768], fi[:, 1536 * h + 768 : 1536 * h + 1536])
    T[0, me.y, me.c, me.z, me.x] = small[...]
    all_here()

    def first_lanes(shape):
        return lax.broadcasted_iota(jnp.int32, shape, 1) < 64

    def two(v):
        keep = first_lanes(v.shape)
        w = f32(v)
        return low(jnp.concatenate([jnp.where(keep, w, 0.0), jnp.where(keep, 0.0, w)], axis=0))

    def one(v):
        return jnp.where(first_lanes((DEC, 128)), v[:DEC], v[DEC:])

    def unpack(src, dst):
        def body(i):
            for z in range(4):
                w = f32(BUF[src, i // 2, i % 2, z])
                for k in range(2):
                    rows = slice(OWN * k, OWN * k + OWN)
                    both = low(jnp.concatenate([w[0, rows], w[1, rows]], axis=0))
                    BUF[dst, k, i // 2, (i % 2) * 2 + z // 2, z % 2] = both

        loop(4, body)

    def whole(b, k):
        return BUF[b, k].reshape(WIDTH, WIDTH)

    def rows_of(i):
        return slice(i * RD, i * RD + RD) if isinstance(i, int) else tile(i, RD)

    def project(a, b, k, dst, i=0):
        r = rows_of(i)
        dst[r, :] = low(dot_nn(a[r, :], whole(b, k)))

    def project_add(a, b, k, base, dst):
        dst[...] = f32(base[...]) + dot_nn(a[...], whole(b, k))

    def norm(v, gain, dst):
        def body(i):
            r = tile(i, 128)
            x = f32(v[r, :])
            s = lax.rsqrt(jnp.mean(x * x, axis=-1, keepdims=True) + EPSILON)
            dst[r, :] = low(x * s * NRM[gain : gain + 1, :])

        loop(RD // 128, body)

    def norm_back(v, gain, G, base, dst):
        def body(i, total):
            r = tile(i, 64)
            x = f32(v[r, :])
            s = lax.rsqrt(jnp.mean(x * x, axis=-1, keepdims=True) + EPSILON)
            n = x * s
            w = G[r, :]
            u = w * NRM[gain : gain + 1, :]
            dst[r, :] = f32(base[r, :]) + s * (u - n * jnp.mean(u * n, axis=-1, keepdims=True))
            return total + jnp.sum((w * n).reshape(8, 8, WIDTH), axis=0)

        total = lax.fori_loop(0, RD // 64, body, jnp.zeros((8, WIDTH), jnp.float32))
        return jnp.sum(total, axis=0, keepdims=True)

    def softmax(s):
        e = jnp.exp(s - jnp.max(s, axis=-1, keepdims=True))
        return e * (1.0 / jnp.sum(e, axis=-1, keepdims=True))

    def attend(q, k, v, o, probs, slots, mask, lo, hi):
        def body(j):
            i = j + lo
            lanes = tile(i, 128)
            for at in range(SEQS):
                r, kr = slice(at * DEC, at * DEC + DEC), slice(at * slots, at * slots + slots)
                s = dot_nt(two(q[r, lanes]), k[kr, lanes])
                p = low(softmax(mask(s, at, i)))
                probs[i, at] = p
                o[r, lanes] = low(one(dot_nn(p, v[kr, lanes])))

        loop(hi - lo, body)

    def attend_back(q, k, v, go, probs, slots, lo, hi, extra):
        def body(j):
            i = j + lo
            lanes = tile(i, 128)
            for at in range(SEQS):
                r, kr = slice(at * DEC, at * DEC + DEC), slice(at * slots, at * slots + slots)
                q2, g2, p = two(q[r, lanes]), two(go[r, lanes]), probs[i, at]
                d = dot_nt(g2, v[kr, lanes])
                pf = f32(p)
                gs = low(pf * (d - jnp.sum(pf * d, axis=-1, keepdims=True)))
                v[kr, lanes] = low(dot_tn(p, g2))
                q[r, lanes] = low(one(dot_nn(gs, k[kr, lanes])))
                k[kr, lanes] = low(dot_tn(gs, q2))
                extra(gs, i)

        loop(hi - lo, body)

    def back_project(pairs, dst, cast, i=0):
        r = rows_of(i)
        v = None
        for a, b, k in pairs:
            d = dot_nt(a[r, :], whole(b, k))
            v = d if v is None else v + d
        dst[r, :] = cast(v)

    def grad_pair(aa, ga, ab, gb, place, oa=0, ob=0, tiles=(0, 1, 2)):
        for n in tiles:
            va = dot_tn(aa[...], ga[:, (n + oa) * BLK : (n + oa + 1) * BLK]).reshape(32, OWN, BLK)
            vb = dot_tn(ab[...], gb[:, (n + ob) * BLK : (n + ob + 1) * BLK]).reshape(32, OWN, BLK)
            both = low(jnp.concatenate([va, vb], axis=1))
            BUF[place, :, :, :, :, :, n * BLK : (n + 1) * BLK] = both.reshape(2, 2, 4, 2, ROWS, BLK)

    owner = jnp.floor((f32(lax.broadcasted_iota(jnp.int32, (1, WIDTH), 1)) + 0.5) * (1.0 / OWN))

    def spread():
        place = f32(lax.broadcasted_iota(jnp.int32, (128, WIDTH), 1)) - OWN * owner
        return low(jnp.where(place == f32(lax.broadcasted_iota(jnp.int32, (128, WIDTH), 0)), 1.0, 0.0))

    row = f32(lax.broadcasted_iota(jnp.int32, (32 * TROWS, 1), 0)) - TROWS * owner
    def self_mask(s, at, pair):
        k = lax.broadcasted_iota(jnp.int32, s.shape, 1)
        q = lax.broadcasted_iota(jnp.int32, s.shape, 0) % DEC
        return jnp.where((k <= q) & (k < dlen[at]), s + BIAS[pair], MASKED)

    def cross_mask(s, at, pair):
        return jnp.where(lax.broadcasted_iota(jnp.int32, s.shape, 1) < elen[at], s, MASKED)

    def out_rows(j):
        return jnp.concatenate([BUF[b, j // 2, j % 2] for b in (5, 6)], axis=2).reshape(WIDTH, WIDTH)

    def feed(j, b):
        k = j % 2
        pre = dot_nn(A3[...], whole(b, k))
        gh = dot_nt(C[...], out_rows(j))
        th = jnp.tanh(GELU * (pre + 0.044715 * (pre * pre * pre)))
        HID[:, j * WIDTH : (j + 1) * WIDTH] = low(0.5 * pre * (1.0 + th))
        slope = 0.5 * (1.0 + th) + 0.5 * pre * (1.0 - th * th) * (GELU * (1.0 + 0.134145 * (pre * pre)))
        GP[:, j * WIDTH : (j + 1) * WIDTH] = low(slope * gh)

    def feed_grads(j):
        for n in range(3):
            w = low(dot_tn(HID[:, j * WIDTH : (j + 1) * WIDTH], C[:, n * BLK : (n + 1) * BLK]))
            w = w.reshape(4, 2, 2 * ROWS, BLK)
            for e in range(2):
                part = w[:, :, ROWS * e : ROWS * e + ROWS]
                BUF[PLACE[2 + e], j // 2, j % 2, :, :, :, n * BLK : (n + 1) * BLK] = part

    def mix_back(j, b):
        d = dot_nt(GP[:, j * WIDTH : (j + 1) * WIDTH], whole(b, j % 2))
        F2[...] = d if j == 0 else F2[...] + d

    def mix():
        v = Y2[...]
        for j in range(4):
            v = v + dot_nn(HID[:, j * WIDTH : (j + 1) * WIDTH], out_rows(j))
        A3[...] = low(v)


    def cast_rows(src, dst):
        def body(i):
            q = tile(i, 64)
            dst[q, :] = low(src[q, :])

        loop(RD // 64, body)

    def nothing(gs, pair):
        pass

    def sum_bias(gs, pair):
        BIAS[pair] += f32(gs)

    def done(*pieces):
        g.drain([u for u, unit in enumerate(GATHERED) if unit[0] - 1 in pieces])

    stores, gains = [], {}

    def store(src, dst, i):
        stores.append(pltpu.make_async_copy(src, dst, lsem.at[i]))
        stores[-1].start()

    def init():
        for cp in loads:
            cp.wait()
        place = lax.broadcasted_iota(jnp.int32, (DEC, WIDTH), 0)
        for s in range(SEQS):
            r = slice(DEC * s, DEC * s + DEC)
            C[r, :] = low(jnp.where(place < dlen[s], f32(C[r, :]), 0.0))

    def tables():
        h.drain()
        table = T[0].reshape(32 * TROWS, 128)
        wide = dot_nn(table, spread())
        NRM[...] = jnp.concatenate(
            [jnp.sum(jnp.where(row == float(n), wide, 0.0), axis=0, keepdims=True) for n in range(3)]
            + [jnp.zeros((5, WIDTH), jnp.float32)],
            axis=0,
        )
        DM[...] = dot_tn(T[0, 0, 0].reshape(8 * TROWS, 128), bmap[...])
        for j in range(2 * PAIRS):
            v = jnp.broadcast_to(DM[j : j + 1, :], (DEC, DEC))
            BIAS[j // 2, DEC * (j % 2) : DEC * (j % 2) + DEC, :] = pltpu.roll(v, 0, 1, stride=1, stride_axis=0)

    def unpack_to(src, dst, *pieces):
        done(*pieces)
        unpack(src, dst)

    def self_out():
        project_add(O1, 1, 1, X, Y1)
        norm(Y1, 1, A2)

    def cross_out():
        project_add(O2, 3, 1, Y1, Y2)
        norm(Y2, 2, A3)

    def in_grads(h):
        if h:
            done(4, 5, 7)
        grad_pair(A3, GP, A3, GP, PLACE[h], 6 * h, 6 * h + 3)

    def finish():
        mix()
        store(A3, out_hbm, 0)

    def norm_back_ffn():
        gains[2] = norm_back(Y2, 2, F2, C, GY)
        cast_rows(GY, C)

    def norm_back_cross():
        gains[1] = norm_back(Y1, 1, F2, GY, GY)
        cast_rows(GY, C)
        BIAS[...] = jnp.zeros_like(BIAS)

    def norm_back_self():
        gains[0] = norm_back(X, 0, F2, GY, GY)
        cast_rows(GY, GO)
        store(GO, gdec_hbm, 1)

    def enc_grad(i):
        loop(2, lambda n: back_project([(K, 2, 0), (V, 2, 1)], E, low, n + 2 * i))
        if i:
            store(E, genc_hbm, 2)

    def small_grads():
        DM[...] = jnp.zeros_like(DM)
        flip = lax.broadcasted_iota(jnp.int32, (DEC, DEC), 0) + lax.broadcasted_iota(jnp.int32, (DEC, DEC), 1)
        flip = low(jnp.where(flip == DEC - 1, 1.0, 0.0))
        for j in range(2 * PAIRS):
            v = BIAS[j // 2, DEC * (j % 2) : DEC * (j % 2) + DEC, :]
            hi = low(v)
            v = dot_nn(flip, hi) + dot_nn(flip, low(v - f32(hi)))
            v = pltpu.roll(v, 0, 1, stride=1, stride_axis=0)
            DM[j : j + 1, :] = jnp.sum(v, axis=0, keepdims=True)
        DM[...] = pltpu.roll(DM[...], 1, 1)
        hi = low(DM[...])
        rel = dot_nt(bmap[...], hi) + dot_nt(bmap[...], low(DM[...] - f32(hi)))
        spots = sum(jnp.where(row == float(n), gains[n], 0.0) for n in range(3))
        spots = dot_nt(low(spots), spread()).reshape(4, 128, 128)
        for d in range(4):
            GT[0, d // 2, d % 2] = low(spots[d] + rel).reshape(4, 2, TROWS, 128)

    def many(n, fn, each=1):
        return [functools.partial(fn, i // each) if i % each == 0 else int for i in range(n)]

    work = [
        init,
        tables,
        lambda: norm(X, 0, A1),
        lambda: (unpack(1, 0), project(A1, 0, 0, Q1)),
        lambda: project(A1, 0, 1, K1),
        lambda: (unpack_to(2, 1, 0), project(A1, 1, 0, V1)),
        *many(3, lambda i: attend(Q1, K1, V1, O1, PS, DEC, self_mask, 0, 6), 3),
        self_out,
        *many(4, lambda i: (None if i else unpack_to(3, 2, 1), loop(2, lambda n: project(E, 2, 0, K, n + 2 * i))), 2),
        *many(4, lambda i: loop(2, lambda n: project(E, 2, 1, V, n + 2 * i)), 2),
        lambda: (unpack_to(4, 3, 2), project(A2, 3, 0, Q2)),
        *many(6, lambda i: attend(Q2, K, V, O2, PC, ENC, cross_mask, 3 * i, 3 * i + 3), 3),
        cross_out,
        lambda: unpack_to(7, 4, 3),
        *many(2, lambda i: feed(i, 4)),
        lambda: in_grads(0),
        lambda: unpack_to(8, 7, 6),
        *many(2, lambda i: feed(2 + i, 7)),
        lambda: in_grads(1),
        *many(4, feed_grads),
        *many(4, lambda j: mix_back(j, 4 if j < 2 else 7)),
        norm_back_ffn,
        lambda: back_project([(C, 3, 1)], GO, low),
        *many(6, lambda i: attend_back(Q2, K, V, GO, PC, ENC, 3 * i, 3 * i + 3, nothing), 3),
        lambda: grad_pair(A2, Q2, O2, C, PLACE[4]),
        *many(3, lambda n: grad_pair(E, K, E, V, PLACE[5], tiles=(n,))),
        finish,
        lambda: back_project([(Q2, 3, 0)], F2, f32),
        norm_back_cross,
        lambda: back_project([(C, 1, 1)], GO, low),
        *many(3, lambda i: attend_back(Q1, K1, V1, GO, PS, DEC, 0, 6, sum_bias), 3),
        lambda: grad_pair(A1, V1, O1, C, PLACE[6]),
        lambda: grad_pair(A1, Q1, A1, K1, PLACE[7]),
        *many(4, enc_grad, 2),
        lambda: back_project([(Q1, 0, 0), (K1, 0, 1), (V1, 1, 0)], F2, f32),
        norm_back_self,
        small_grads,
    ]
    rows_g, rows_r, last = sem_rows([unit[0] - 1 for unit in GATHERED], [unit[0] for unit in REDUCED])
    g = Gather(me, BUF, ss, rs, rows_g)
    h = Gather(me, T, ss, rs, rows_g)
    r = Reduce(me, BUF, RC, gw, ss, rs, rows_r, ready, free, SLOTS, NP)
    rt = Reduce(me, GT, RCT, gt, ss, rs, rows_r, tready, tfree, 1, 1)
    na, nr = len(GATHERED), len(REDUCED)
    gathers = [g.steps(u, *unit) for u, unit in enumerate(GATHERED)] + [h.steps(na, 0, 0, 128, "zyx")]
    parts = [sum(unit[0] == p for unit in REDUCED) for p in range(NP)]
    reduces = [r.steps(u, p, PLACE[p], *cut, parts[p]) for u, (p, *cut) in enumerate(REDUCED)]
    reduces.append(rt.steps(nr, 0, 0, 0, 128, "xyz", 1))
    for code in PLAN:
        if code >= 2000:
            work[code - 2000]()
        else:
            (reduces if code >= 1000 else gathers)[code % 1000 // 10][code % 10]()
    g.drain()
    h.drain()
    r.drain()
    rt.drain()
    for cp in stores:
        cp.wait()


def layer_here(shards, dec_in, enc_out, dec_len, enc_len, cotangent):
    ns, sq, sk, sv, so, rel, nc, cq, ck, cv, co, nf, fi, fo = shards
    gains = jnp.pad(jnp.stack([ns, nc, nf]), ((0, 1), (0, 128 - OWN)))
    small = jnp.concatenate([gains, jnp.pad(rel, ((0, 8), (0, 128 - rel.shape[1])))], axis=0)
    b16, w32 = jnp.bfloat16, jnp.float32

    def vm(shape, dtype=b16):
        return pltpu.VMEM(shape, dtype)

    dec, enc = (RD, WIDTH), (RE, WIDTH)
    scratch = [
        vm((12, *CHUNKS, ROWS, COLS)),
        vm((1, *CHUNKS, TROWS, 128)),
        vm((1, *CHUNKS, TROWS, 128)),
        vm((1, 2, 4, 2, TROWS, 128)),
        vm((SLOTS, 2, 4, 2, ROWS, COLS)),
        vm(dec), vm(dec), vm(enc), vm(enc), vm(enc),
        *[vm(dec)] * 10,
        *[vm((RD, 4 * WIDTH))] * 2,
        *[vm(dec, w32)] * 4,
        vm((PAIRS, SEQS, 2 * DEC, DEC)),
        vm((PAIRS, SEQS, 2 * DEC, ENC)),
        vm((PAIRS, 2 * DEC, DEC), w32),
        vm((8, WIDTH), w32),
        vm((128, 128), w32),
        *[pltpu.SemaphoreType.DMA((sem_rows([u[0] - 1 for u in GATHERED], [u[0] for u in REDUCED])[2] + 1, 6))] * 2,
        pltpu.SemaphoreType.REGULAR((NP, 5)),
        pltpu.SemaphoreType.REGULAR((NP,)),
        pltpu.SemaphoreType.REGULAR((1, 5)),
        pltpu.SemaphoreType.REGULAR((1,)),
        pltpu.SemaphoreType.DMA((3,)),
    ]
    here, away = pl.BlockSpec(memory_space=pltpu.VMEM), pl.BlockSpec(memory_space=pl.ANY)
    scalars = pl.BlockSpec(memory_space=pltpu.SMEM)
    out, g_dec, g_enc, gw, gt = pl.pallas_call(
        layer_kernel,
        out_shape=(
            jax.ShapeDtypeStruct(dec, b16),
            jax.ShapeDtypeStruct(dec, b16),
            jax.ShapeDtypeStruct(enc, b16),
            jax.ShapeDtypeStruct((NP, ROWS, COLS), w32),
            jax.ShapeDtypeStruct((1, TROWS, 128), w32),
        ),
        in_specs=[scalars] * 2 + [away] * 3 + [here] * 12,
        out_specs=[away] * 3 + [here] * 2,
        scratch_shapes=scratch,
        compiler_params=pltpu.CompilerParams(
            collective_id=0, has_side_effects=True, vmem_limit_bytes=60 * 2**20
        ),
    )(
        dec_len.reshape(-1), enc_len.reshape(-1),
        dec_in.reshape(dec), enc_out.reshape(enc), cotangent.reshape(dec),
        small, bucket_rows(), sq, sk, sv, so, cq, ck, cv, co, fi, fo,
    )
    return deliver(out, g_dec, g_enc, gw, gt, rel.shape)


def deliver_kernel(out, gdec, genc, gw, gt, o0, o1, o2, *outs):
    grads, (w_fi, w_fo, n1, n2, n3, rel, sem) = outs[:8], outs[8:]
    moves = [(out, o0), (gdec, o1), (genc, o2)]
    at = ((7, 0), (7, 1), (6, 0), (6, 1), (4, 0), (5, 0), (5, 1), (4, 1))
    moves += [(gw.at[p, pl.ds(OWN * h, OWN)], o) for (p, h), o in zip(at, grads)]
    for j in range(4):
        moves.append((gw.at[j // 2, pl.ds(OWN * (j % 2), OWN)], w_fi.at[:, pl.ds(WIDTH * j, WIDTH)]))
    moves += [(gw.at[2 + e], w_fo.at[pl.ds(ROWS * e, ROWS)]) for e in range(2)]
    copies = [pltpu.make_async_copy(a, b, sem.at[i]) for i, (a, b) in enumerate(moves)]
    for cp in copies:
        cp.start()
    for n, o in enumerate((n1, n2, n3)):
        o[...] = gt[0, n : n + 1, :OWN]
    rel[...] = gt[0, 4 : 4 + rel.shape[0], : rel.shape[1]]
    for cp in copies:
        cp.wait()


def deliver(out, g_dec, g_enc, gw, gt, rel):
    here, away = pl.BlockSpec(memory_space=pltpu.VMEM), pl.BlockSpec(memory_space=pl.ANY)
    w32 = [(OWN, WIDTH)] * 8 + [(OWN, 4 * WIDTH), (2 * ROWS, WIDTH)] + [(1, OWN)] * 3 + [rel]
    got = pl.pallas_call(
        deliver_kernel,
        out_shape=[jax.ShapeDtypeStruct(v.shape, v.dtype) for v in (out, g_dec, g_enc)]
        + [jax.ShapeDtypeStruct(v, jnp.float32) for v in w32],
        in_specs=[away] * 4 + [here],
        out_specs=[here] * 17,
        scratch_shapes=[pltpu.SemaphoreType.DMA((17,))],
    )(out, g_dec, g_enc, gw, gt)
    sq, sk, sv, so, cq, ck, cv, co, w_fi, w_fo, n1, n2, n3, w_rel = got[3:]
    n1, n2, n3 = (v.reshape(-1) for v in (n1, n2, n3))
    return got[0], got[1], got[2], (n1, sq, sk, sv, so, w_rel, n2, cq, ck, cv, co, n3, w_fi, w_fo)


EPSILON = 1e-06
MASKED = -1000000000.0
NB = 32
AT = ("dp", "fsdp")


def bucket_table(dec_slots, bucket_count):
    near = bucket_count // 2
    places = np.arange(dec_slots, dtype=np.int32)
    distance = np.maximum(places[:, None] - places[None, :], 0).astype(np.int32)
    edges = np.array(
        [math.ceil(near * (128 / near) ** (level / near) - 1e-09) for level in range(1, near)],
        dtype=np.int32,
    )
    far = near + np.sum(
        (distance[:, :, None] >= edges[None, None, :]).astype(np.int32), axis=-1, dtype=np.int32
    )
    return np.where(distance < near, distance, far).astype(np.int32)


def rms_norm(values, gain):
    return values * lax.rsqrt(jnp.mean(values * values, axis=-1, keepdims=True) + EPSILON) * gain


def smooth(values):
    return jax.nn.gelu(values, approximate=True)


def dot_nn(a, b):
    return jnp.dot(a, b, preferred_element_type=jnp.float32)


def dot_nt(a, b):
    return lax.dot_general(a, b, (((1,), (1,)), ((), ())), preferred_element_type=jnp.float32)


def dot_tn(a, b):
    return lax.dot_general(a, b, (((0,), (0,)), ((), ())), preferred_element_type=jnp.float32)


def low(v):
    return v.astype(jnp.bfloat16)


def layer_plain(weights, dec_rows, enc_rows, dec_len, enc_len, cot_rows):
    ns, sq, sk, sv, so, rel, nc, cq, ck, cv, co, nf, fi, fo = weights
    seqs, dec_slots, width = dec_rows.shape
    enc_slots = enc_rows.shape[1]
    heads = rel.shape[1]
    size = width // heads
    ns, nc, nf = (v.astype(jnp.float32) for v in (ns, nc, nf))
    places = jnp.arange(dec_slots, dtype=jnp.int32)
    causal = places[None, :] <= places[:, None]
    self_mask = causal[None, None] & (places[None, None, None, :] < dec_len[:, None, None, None])
    enc_places = jnp.arange(enc_slots, dtype=jnp.int32)
    cross_mask = enc_places[None, None, None, :] < enc_len[:, None, None, None]
    row_mask = (places[None, :] < dec_len[:, None]).astype(jnp.float32)
    table = bucket_table(dec_slots, NB).reshape(-1)
    onehot = jnp.asarray((table[:, None] == np.arange(NB)[None, :]).astype(np.float32), jnp.bfloat16)
    bias = lax.dot_general(rel, onehot, (((0,), (1,)), ((), ())), preferred_element_type=jnp.float32)
    bias = bias.reshape(heads, dec_slots, dec_slots)[None]

    def split(t):
        return t.reshape(seqs, -1, heads, size).transpose(0, 2, 1, 3)

    def join(t):
        return t.transpose(0, 2, 1, 3).reshape(-1, width)

    def many(a, b, ca, cb):
        return lax.dot_general(
            a, b, (((ca,), (cb,)), ((0, 1), (0, 1))), preferred_element_type=jnp.float32
        )

    def attend(q, k, v, add, mask):
        s = jnp.where(mask, many(q, k, 3, 3) + add, MASKED)
        top = jnp.max(s, axis=-1, keepdims=True)
        e = jnp.exp(s - top)
        p = e / jnp.sum(e, axis=-1, keepdims=True)
        return p, low(many(low(p), v, 3, 2))

    def back(q, k, v, p, g):
        gv = low(many(low(p), g, 2, 2))
        d = many(g, v, 3, 3)
        gs = low(p * (d - jnp.sum(p * d, axis=-1, keepdims=True)))
        return low(many(gs, k, 3, 2)), low(many(gs, q, 2, 2)), gv, gs

    x = dec_rows.reshape(-1, width).astype(jnp.float32)
    enc = enc_rows.reshape(-1, width)
    a1 = low(rms_norm(x, ns))
    q1, k1, v1 = (split(low(dot_nn(a1, w))) for w in (sq, sk, sv))
    p1, o1 = attend(q1, k1, v1, bias, self_mask)
    o1 = join(o1)
    y1 = x + dot_nn(o1, so)
    a2 = low(rms_norm(y1, nc))
    q2 = split(low(dot_nn(a2, cq)))
    k2, v2 = (split(low(dot_nn(enc, w))) for w in (ck, cv))
    p2, o2 = attend(q2, k2, v2, 0.0, cross_mask)
    o2 = join(o2)
    y2 = y1 + dot_nn(o2, co)
    a3 = low(rms_norm(y2, nf))
    pre = dot_nn(a3, fi)
    hidden = low(smooth(pre))
    out = y2 + dot_nn(hidden, fo)
    g = (cot_rows.astype(jnp.float32) * row_mask[:, :, None]).reshape(-1, width)
    gf = low(g)
    w_fo = dot_tn(hidden, gf)
    gp = low(jax.vjp(smooth, pre)[1](dot_nt(gf, fo))[0])
    w_fi = dot_tn(a3, gp)
    part, w_nf = jax.vjp(rms_norm, y2, nf)[1](dot_nt(gp, fi))
    gy = g + part
    gc = low(gy)
    w_co = dot_tn(o2, gc)
    gq, gk, gv, _ = back(q2, k2, v2, p2, split(low(dot_nt(gc, co))))
    gq, gk, gv = join(gq), join(gk), join(gv)
    w_cq, w_ck, w_cv = dot_tn(a2, gq), dot_tn(enc, gk), dot_tn(enc, gv)
    g_enc = dot_nt(gk, ck) + dot_nt(gv, cv)
    part, w_nc = jax.vjp(rms_norm, y1, nc)[1](dot_nt(gq, cq))
    gy = gy + part
    ga = low(gy)
    w_so = dot_tn(o1, ga)
    gq, gk, gv, gs = back(q1, k1, v1, p1, split(low(dot_nt(ga, so))))
    w_rel = lax.dot_general(
        onehot, gs.reshape(seqs, heads, -1), (((0,), (2,)), ((), ())), preferred_element_type=jnp.float32
    ).sum(axis=1)
    gq, gk, gv = join(gq), join(gk), join(gv)
    w_sq, w_sk, w_sv = dot_tn(a1, gq), dot_tn(a1, gk), dot_tn(a1, gv)
    part, w_ns = jax.vjp(rms_norm, x, ns)[1](dot_nt(gq, sq) + dot_nt(gk, sk) + dot_nt(gv, sv))
    grads = (w_ns, w_sq, w_sk, w_sv, w_so, w_rel, w_nc, w_cq, w_ck, w_cv, w_co, w_nf, w_fi, w_fo)
    return low(out), low(gy + part), low(g_enc), grads


REL = 5


def on_device(dec_in, enc_out, dec_len, enc_len, cotangent, *shards):
    micro, per, dec_slots, width = dec_in.shape
    seqs, enc_slots = micro * per, enc_out.shape[2]
    if (lax.axis_size("dp"), lax.axis_size("fsdp"), seqs, dec_slots, enc_slots, width) == HERE:
        out, g_dec, g_enc, grads = layer_here(shards, dec_in, enc_out, dec_len, enc_len, cotangent)
    else:
        whole = [lax.all_gather(w, AT[1] if i == REL else AT, axis=0, tiled=True) for i, w in enumerate(shards)]
        out, g_dec, g_enc, grads = layer_plain(
            whole,
            dec_in.reshape(seqs, dec_slots, width),
            enc_out.reshape(seqs, enc_slots, width),
            dec_len.reshape(-1),
            enc_len.reshape(-1),
            cotangent.reshape(seqs, dec_slots, width),
        )
        grads = [
            lax.psum_scatter(
                lax.psum(w, AT[0]) if i == REL else w,
                AT[1] if i == REL else AT,
                scatter_dimension=0,
                tiled=True,
            )
            for i, w in enumerate(grads)
        ]
    return (out.reshape(dec_in.shape), g_dec.reshape(dec_in.shape), g_enc.reshape(enc_out.shape), *grads)


def solution(mesh):
    rows, seq = P(AT, None), P(None, AT, None, None)
    gain, lens, rel = P(AT), P(None, AT), P(AT[1], None)
    placed = (gain, rows, rows, rows, rows, rel, gain, rows, rows, rows, rows, gain, rows, rows)
    return jax.shard_map(
        on_device,
        mesh=mesh,
        in_specs=(seq, seq, lens, lens, seq, *placed),
        out_specs=(seq, seq, seq, *placed),
        check_vma=False,
    )
```

profile of v0, /device:TPU:0, one launch (start us, length us, event | category | flops | bytes accessed | tf_op | source)
XLA Modules:
  0.0 190.9 jit_solution(8267169512984660615)
XLA Ops:
  0.7 0.7 fusion.8
  1.4 1.3 fusion.1.small
  2.6 183.5 %shard_map.323 = (bf16[256,768]{1,0:T(8,128)(2,1)}, bf16[256,768]{1,0:T(8,128)(2,1)}, bf16[1024,768]{1,0:T(8,128)(2,1)}, f32[8,48,768]{2,1,0:T(8,128)}, f32[1,16,128]{2,1,0:T(8,128)}) custom-call(s32[2]{0:T(128)} %bitcast.26, s32[2]{0:T(128)} %bitcast.27, bf16[256,768]{1,0:T(8,128)(2,1)} %bitcast.21, bf16[1024,768]{1,0:T(8,128)(2,1)} %bitcast.20, ...), custom_call_target="tpu_custom_call" | custom-call | tf_op jit(solution)/shard_map/pallas_call | solution.py:725
  186.1 4.6 %shard_map.324 = (bf16[256,768]{1,0:T(8,128)(2,1)}, bf16[256,768]{1,0:T(8,128)(2,1)}, bf16[1024,768]{1,0:T(8,128)(2,1)}, f32[24,768]{1,0:T(8,128)}, f32[24,768]{...) custom-call(bf16[256,768]{1,0:T(8,128)(2,1)} %get-tuple-element.39.o, ...), custom_call_target="tpu_custom_call" | custom-call | tf_op jit(solution)/shard_map/pallas_call | solution.py:769
where the time goes:
time: 191 us
  Pallas kernels  188 us (98%)
  other arithmetic  1.98 us (1%)
    pallas_call x1, Pallas kernels, layer_here(): pl.pallas_call(layer_kernel, out_shape=(jax.ShapeDtypeStruct(dec, b16), j...  183 us
    pallas_call x1, Pallas kernels, deliver(): pl.pallas_call(deliver_kernel, out_shape=[jax.ShapeDtypeStruct(v.shape, v...  4.59 us

commit v1 on v0

--- a/solution.py
+++ b/solution.py
@@ -229,42 +229,42 @@
 GELU = math.sqrt(2.0 / math.pi)
 PLACE = (9, 8, 10, 11, 4, 7, 5, 6)
 GATHERED = (
-    (1, 0, 128, "zyx"),
+    (1, 0, 128, "zxy"),
     (1, 128, 512, "zyx"),
     (1, 640, 128, "zyx"),
     (2, 0, 384, "zxy"),
     (2, 384, 256, "yzx"),
     (2, 640, 128, "zyx"),
-    (3, 0, 256, "zxy"),
-    (3, 256, 384, "zxy"),
-    (3, 640, 128, "zyx"),
+    (3, 0, 128, "zxy"),
+    (3, 128, 384, "zxy"),
+    (3, 512, 256, "zyx"),
     (4, 0, 512, "xzy"),
-    (4, 512, 128, "zyx"),
-    (4, 640, 128, "zxy"),
-    (5, 0, 384, "zyx"),
-    (5, 384, 256, "xzy"),
-    (5, 640, 128, "yxz"),
+    (4, 512, 128, "zxy"),
+    (4, 640, 128, "zyx"),
+    (5, 0, 256, "zyx"),
+    (5, 256, 256, "xzy"),
+    (5, 512, 256, "xzy"),
     (6, 0, 384, "yzx"),
     (6, 384, 256, "zyx"),
     (6, 640, 128, "xzy"),
-    (7, 0, 512, "zxy"),
-    (7, 512, 128, "xyz"),
-    (7, 640, 128, "zyx"),
+    (7, 0, 256, "zxy"),
+    (7, 256, 128, "yxz"),
+    (7, 384, 384, "zyx"),
     (8, 0, 256, "zxy"),
     (8, 256, 256, "xyz"),
     (8, 512, 256, "zyx"),
 )
 REDUCED = (
-    (0, 0, 384, "xyz"),
-    (0, 384, 256, "yxz"),
-    (0, 640, 128, "zxy"),
-    (1, 0, 256, "xyz"),
-    (1, 256, 384, "yxz"),
+    (0, 0, 512, "xyz"),
+    (0, 512, 256, "yxz"),
+    (1, 0, 512, "xyz"),
+    (1, 512, 128, "yxz"),
     (1, 640, 128, "zxy"),
-    (2, 0, 640, "xyz"),
+    (2, 0, 384, "xyz"),
+    (2, 384, 256, "yxz"),
     (2, 640, 128, "zxy"),
     (3, 0, 640, "yxz"),
-    (3, 640, 128, "zyx"),
+    (3, 640, 128, "zxy"),
     (4, 0, 384, "xyz"),
     (4, 384, 256, "yxz"),
     (4, 640, 128, "zyx"),
@@ -273,32 +273,32 @@
     (5, 640, 128, "zyx"),
     (6, 0, 256, "xyz"),
     (6, 256, 384, "yxz"),
-    (6, 640, 128, "zyx"),
-    (7, 0, 384, "xyz"),
-    (7, 384, 384, "yxz"),
+    (6, 640, 128, "zxy"),
+    (7, 0, 512, "xyz"),
+    (7, 512, 256, "yxz"),
 )
 PLAN = (
-    240, 2000, 90, 100, 110, 0, 10, 20, 60, 241, 70, 80, 91, 101, 242, 111,
-    1, 102, 243, 112, 244, 2001, 11, 21, 2, 103, 2002, 61, 113, 104, 30, 40,
-    50, 114, 71, 3, 81, 4, 12, 62, 22, 41, 82, 72, 150, 160, 170, 63,
-    92, 64, 120, 130, 140, 31, 51, 13, 73, 180, 190, 200, 23, 14, 151, 74,
-    24, 2003, 42, 83, 171, 131, 161, 2004, 84, 210, 220, 230, 32, 191, 121, 93,
-    141, 52, 43, 94, 221, 181, 142, 162, 201, 44, 53, 54, 33, 182, 192, 152,
-    34, 2005, 172, 2006, 122, 2007, 222, 163, 2008, 202, 2009, 132, 164, 2010, 2011, 2012,
-    211, 2013, 2014, 2015, 231, 2016, 153, 2017, 2018, 2019, 154, 2020, 183, 2021, 143, 2022,
-    173, 2023, 123, 144, 184, 2024, 174, 2025, 193, 124, 203, 133, 194, 212, 204, 134,
-    2026, 232, 2027, 2028, 2029, 1000, 1010, 1020, 1001, 213, 1011, 1021, 223, 233, 1002, 214,
-    1012, 1022, 224, 234, 2030, 2031, 2032, 2033, 1030, 1040, 1050, 2034, 1031, 2035, 2036, 1013,
-    1041, 1051, 2037, 1060, 1070, 1080, 1090, 1003, 1032, 2038, 2039, 1061, 1023, 1071, 1042, 1052,
-    1014, 1081, 1091, 2040, 1062, 1072, 1004, 1082, 1092, 1033, 1024, 2041, 2042, 2043, 2044, 2045,
-    2046, 1043, 1053, 2047, 2048, 1015, 2049, 2050, 1100, 1110, 1120, 2051, 1101, 2052, 1063, 1073,
-    1111, 1121, 2053, 1130, 1140, 1150, 1102, 1044, 1005, 1083, 1074, 1131, 1141, 1151, 1054, 1112,
-    1122, 1034, 1025, 2054, 1132, 1142, 1152, 1093, 2055, 2056, 1075, 1064, 1045, 1055, 1103, 2057,
-    2058, 2059, 2060, 2061, 1113, 1123, 1084, 1035, 1160, 1170, 1180, 2062, 1190, 1200, 1161, 2063,
-    1171, 1181, 1143, 2064, 1094, 1191, 1162, 1153, 1201, 1172, 1182, 1133, 1192, 1104, 1202, 1154,
-    1114, 1124, 2065, 2066, 1065, 1144, 1095, 2067, 2068, 2069, 1085, 1163, 1173, 1210, 1211, 1134,
-    1183, 1212, 1193, 1155, 1125, 1105, 1115, 1203, 1174, 1213, 1145, 1164, 1184, 1135, 1194, 1204,
-    1185, 1214, 1175, 1165, 1195, 1205, 1215,
+    240, 90, 100, 110, 2000, 0, 10, 20, 60, 70, 80, 241, 91, 101, 111, 242,
+    1, 102, 30, 243, 40, 50, 112, 2, 244, 2001, 11, 21, 41, 61, 103, 113,
+    2002, 3, 104, 114, 71, 4, 62, 81, 12, 22, 72, 63, 64, 82, 150, 160,
+    170, 92, 31, 180, 13, 51, 73, 190, 200, 120, 130, 140, 151, 23, 14, 74,
+    24, 2003, 42, 2004, 161, 83, 171, 84, 181, 32, 93, 131, 141, 52, 191, 201,
+    94, 162, 121, 210, 220, 230, 43, 44, 182, 53, 33, 192, 54, 152, 34, 2005,
+    172, 202, 2006, 221, 122, 163, 2007, 2008, 2009, 2010, 132, 164, 2011, 2012, 2013, 2014,
+    183, 2015, 2016, 142, 153, 173, 2017, 2018, 222, 211, 184, 2019, 231, 154, 174, 2020,
+    2021, 2022, 133, 203, 2023, 2024, 2025, 193, 134, 143, 204, 123, 194, 144, 232, 124,
+    2026, 212, 2027, 2028, 2029, 1000, 1010, 1001, 223, 1011, 233, 213, 224, 1002, 234, 1012,
+    214, 2030, 2031, 2032, 2033, 1020, 1030, 1040, 2034, 2035, 2036, 1021, 1031, 2037, 1013, 1050,
+    1060, 1070, 1080, 1090, 1041, 2038, 1051, 2039, 1061, 1022, 1071, 1032, 1042, 1003, 1052, 1062,
+    1072, 1014, 1081, 1091, 2040, 2041, 2042, 1033, 2043, 1082, 1092, 2044, 1004, 1043, 2045, 2046,
+    2047, 1063, 1023, 2048, 2049, 2050, 1073, 1100, 1110, 1120, 2051, 1015, 1101, 2052, 1053, 1111,
+    1121, 2053, 1034, 1044, 1102, 1130, 1140, 1150, 1112, 1064, 1093, 1074, 1131, 1141, 1122, 1151,
+    2054, 1083, 1005, 1132, 1035, 1142, 1152, 2055, 1065, 2056, 1024, 1103, 2057, 1094, 2058, 1054,
+    1045, 1123, 2059, 2060, 2061, 1160, 1170, 1180, 2062, 1084, 1075, 1113, 1190, 1200, 1161, 1153,
+    1171, 1181, 2063, 1191, 1201, 1162, 1172, 1143, 1182, 1025, 1133, 1192, 1202, 2064, 2065, 1055,
+    1095, 1154, 1104, 1114, 1124, 2066, 2067, 2068, 1163, 2069, 1085, 1144, 1173, 1210, 1211, 1183,
+    1134, 1212, 1105, 1193, 1155, 1203, 1115, 1125, 1145, 1164, 1174, 1184, 1213, 1135, 1194, 1204,
+    1185, 1214, 1165, 1175, 1195, 1205, 1215,
 )
 
 

time: 191 us -> 191 us (level)
  no operation moved by 1% of the time
where the time goes in v1:
time: 191 us; the launch traced here: 190 us
  Pallas kernels  187 us (98%)
  other arithmetic  1.98 us (1%)
    pallas_call x1, Pallas kernels, layer_here(): pl.pallas_call(layer_kernel, out_shape=(jax.ShapeDtypeStruct(dec, b16), j...  183 us
    pallas_call x1, Pallas kernels, deliver(): pl.pallas_call(deliver_kernel, out_shape=[jax.ShapeDtypeStruct(v.shape, v...  4.59 us

profile of v1, /device:TPU:0, one launch (start us, length us, event | category | flops | bytes accessed | tf_op | source)
XLA Modules:
  0.0 190.3 jit_solution(10556831907282862739)
XLA Ops:
  0.7 0.7 fusion.8
  1.4 1.3 fusion.1.small
  2.6 182.9 %shard_map.323 = (bf16[256,768]{1,0:T(8,128)(2,1)}, bf16[256,768]{1,0:T(8,128)(2,1)}, bf16[1024,768]{1,0:T(8,128)(2,1)}, f32[8,48,768]{2,1,0:T(8,128)}, f32[1,16,128]{2,1,0:T(8,128)}) custom-call(s32[2]{0:T(128)} %bitcast.26, s32[2]{0:T(128)} %bitcast.27, bf16[256,768]{1,0:T(8,128)(2,1)} %bitcast.21, bf16[1024,768]{1,0:T(8,128)(2,1)} %bitcast.20, ...), custom_call_target="tpu_custom_call" | custom-call | tf_op jit(solution)/shard_map/pallas_call | solution.py:725
  185.5 4.6 %shard_map.324 = (bf16[256,768]{1,0:T(8,128)(2,1)}, bf16[256,768]{1,0:T(8,128)(2,1)}, bf16[1024,768]{1,0:T(8,128)(2,1)}, f32[24,768]{1,0:T(8,128)}, f32[24,768]{...) custom-call(bf16[256,768]{1,0:T(8,128)(2,1)} %get-tuple-element.39.o, ...), custom_call_target="tpu_custom_call" | custom-call | tf_op jit(solution)/shard_map/pallas_call | solution.py:769
